TPU v7x, 512 devices: a whole 4x8x8 slice. The times are simulated.
512 devices in a mesh: grp: 16 (over y, x_hi), emb: 32 (over z, x_lo, core).
Axes of the slice: x: 4 (x_hi: 2, x_lo: 2; x = x_hi * 2 + x_lo), y: 8, z: 8, core: 2. Of those that a mesh axis runs over, the one named last changes fastest.
Arguments:
- pooled: bfloat16 [6144, 256, 192], P(('grp', 'emb')), may hold values from -6 to 6
- upstream: bfloat16 [6144, 256, 192], P(('grp', 'emb')), may hold values from -6 to 6
- ids_now: int32 [6144, 256], P(('grp', 'emb')), may hold values from 0 to 511
- ids_next: int32 [6144, 256], P(('grp', 'emb')), may hold values from 0 to 511
- tables: bfloat16 [256, 512, 192], P('emb'), may hold values from -6 to 6
- w_fm: bfloat16 [256, 128], replicated, may hold values from -0.02734375 to 0.02734375
- w_proj: bfloat16 [128, 192], replicated, may hold values from -0.5 to 0.5
- w_lcb: bfloat16 [256, 256], replicated, may hold values from -0.375 to 0.375
- gain: float32 [192], replicated, may hold values from 0.5 to 1.5
Outputs:
- next_rows: bfloat16 [6144, 256, 192], P(('grp', 'emb'))
- table_grad: float32 [256, 512, 192], P('emb', 'grp')
- grad_fm: float32 [256, 128], replicated
- grad_proj: float32 [128, 192], replicated
- grad_lcb: float32 [256, 256], replicated
- grad_gain: float32 [192], replicated
All inputs are finite; a program needn't handle non-finite values.
Results may differ from a plain program's by a relative error of at most 0.017.
Values may be sent and summed in bfloat16 or wider, within the bound.
A program may use at most 64 MiB of HBM per device.

v0:
```python
import jax
import jax.numpy as jnp
from jax import lax
from jax.sharding import PartitionSpec as P


def product(form, left, right):
    return jnp.einsum(form, left, right, preferred_element_type=jnp.float32)


def layer_backward(embeds, cotangent, w_fm, w_proj, w_lcb, gain):
    fm_proj = product("bfc,fj->bcj", embeds, w_fm).astype(jnp.bfloat16)
    fm_rows = product("bfc,bcj->bfj", embeds, fm_proj).astype(jnp.bfloat16)
    projected = product("bfj,jc->bfc", fm_rows, w_proj)
    compressed = product("fi,bfc->bic", w_lcb, embeds)
    summed = embeds.astype(jnp.float32) + projected + compressed
    centre = jnp.mean(summed, axis=2, keepdims=True)
    spread = jnp.mean((summed - centre) ** 2, axis=2, keepdims=True)
    inverse = lax.rsqrt(spread + 1e-05)
    normed = (summed - centre) * inverse
    upper = cotangent.astype(jnp.float32)
    scaled = upper * gain
    grad_sum = inverse * (
        scaled
        - jnp.mean(scaled, axis=2, keepdims=True)
        - normed * jnp.mean(scaled * normed, axis=2, keepdims=True)
    )
    grad_sum = grad_sum.astype(jnp.bfloat16)
    grad_gain = jnp.sum(upper * normed, axis=(0, 1))
    grad_proj = product("bfj,bfc->jc", fm_rows, grad_sum)
    grad_rows = product("bfc,jc->bfj", grad_sum, w_proj).astype(jnp.bfloat16)
    grad_p = product("bfc,bfj->bcj", embeds, grad_rows).astype(jnp.bfloat16)
    grad_fm = product("bfc,bcj->fj", embeds, grad_p)
    grad_lcb = product("bfc,bic->fi", embeds, grad_sum)
    grad_in = (
        grad_sum.astype(jnp.float32)
        + product("bfj,bcj->bfc", grad_rows, fm_proj)
        + product("fj,bcj->bfc", w_fm, grad_p)
        + product("fi,bic->bfc", w_lcb, grad_sum)
    )
    return (grad_in.astype(jnp.bfloat16), (grad_fm, grad_proj, grad_lcb, grad_gain))


def local(pooled, upstream, ids_now, ids_next, tables, w_fm, w_proj, w_lcb, gain):
    samples = pooled.shape[0] * lax.axis_size("grp") * lax.axis_size("emb")
    now_seen, next_seen = (
        lax.all_to_all(ids_now, "emb", split_axis=1, concat_axis=0, tiled=True),
        lax.all_to_all(ids_next, "emb", split_axis=1, concat_axis=0, tiled=True),
    )
    local_features = tables.shape[0]
    row_count = tables.shape[1]
    feature_pos = jnp.arange(local_features)[None, :]
    fetched = tables[feature_pos, next_seen]
    next_rows = lax.all_to_all(fetched, "emb", split_axis=0, concat_axis=1, tiled=True)
    grad_in, partials = layer_backward(pooled, upstream, w_fm, w_proj, w_lcb, gain)
    grad_fm, grad_proj, grad_lcb, grad_gain = partials
    row_index = jnp.arange(row_count)
    indicator = (now_seen.T[:, None, :] == row_index[None, :, None]).astype(jnp.bfloat16)
    table_terms = product(
        "frs,sfc->frc",
        indicator,
        lax.all_to_all(grad_in, "emb", split_axis=1, concat_axis=0, tiled=True),
    )
    table_grad = lax.psum_scatter(
        table_terms.astype(jnp.bfloat16), "grp", scatter_dimension=1, tiled=True
    ).astype(jnp.float32)
    total_fm, total_proj, total_lcb, total_gain = lax.psum(
        (grad_fm, grad_proj, grad_lcb, grad_gain), ("grp", "emb")
    )
    factor = 1.0 / samples
    return (
        next_rows,
        table_grad,
        total_fm * factor,
        total_proj * factor,
        total_lcb * factor,
        total_gain * factor,
    )


def solution(mesh):
    return jax.shard_map(
        local,
        mesh=mesh,
        in_specs=(
            P(("grp", "emb"), None, None),
            P(("grp", "emb"), None, None),
            P(("grp", "emb"), None),
            P(("grp", "emb"), None),
            P("emb", None, None),
            P(),
            P(),
            P(),
            P(),
        ),
        out_specs=(P(("grp", "emb"), None, None), P("emb", "grp", None), P(), P(), P(), P()),
        check_vma=False,
    )
```

profile of v0, /device:TPU:6, one launch (start us, length us, event | category | flops | bytes accessed | tf_op | source)
XLA Modules:
  0.0 348.4 jit_solution(15121220163661007803)
XLA Ops:
  8.0 0.0 copy-start
  8.0 0.0 copy-start.1
  8.0 1.6 copy.66
  9.6 11.9 %all-to-all-start.2 = ((s32[12,32,8]{0,2,1:T(8,128)}), s32[12,32,8]{0,2,1:T(8,128)S(1)}, u32[]{:S(2)}, u32[]{:S(2)}) async-start(s32[12,32,8]{0,2,1:T(8,128)} %bitcast.6), calls=%async_computation.2 | async-start | bytes 262144 | tf_op jit(solution)/shard_map/all_to_all | solution.py:47
  21.6 1.7 convolution_convert_fusion.3
  23.3 0.0 copy-done.1
  23.3 0.4 fusion.13
  23.7 0.0 copy-done
  23.7 0.0 copy-start.5
  23.7 0.5 fusion.17
  24.2 0.3 copy-done.5
  24.5 0.6 fusion.27
  25.1 0.0 copy-start.3
  25.1 0.0 copy-start.8
  25.1 0.3 multiply_reduce_fusion
  25.4 1.0 copy-done.3
  26.4 0.0 copy-done.8
  26.4 1.1 fusion.9
  27.5 0.8 fusion.7
  28.3 0.6 convolution_convert_fusion
  29.0 0.5 fusion.15
  29.5 0.0 copy-start.4
  29.5 0.5 fusion.14
  29.9 0.0 copy-start.2
  29.9 0.8 copy-done.2
  30.8 0.5 fusion.19
  31.2 1.6 fusion.10
  32.8 4.4 %copy.55 = bf16[12,256,192]{2,0,1:T(8,128)(2,1)} copy(bf16[12,256,192]{1,2,0:T(8,128)(2,1)} %fusion.10) | data formatting | bytes 2359296 | tf_op jit(solution)/shard_map/convert_element_type | solution.py:41
  37.2 0.0 all-to-all-done.2
  37.2 8.3 %all-to-all-start.3 = ((bf16[12,256,192]{2,0,1:T(8,128)(2,1)}), bf16[12,256,192]{2,0,1:T(8,128)(2,1)}, u32[]{:S(2)}, u32[]{:S(2)}) async-start(bf16[12,256,192]{2,0,1:T(8,128)(2,1)} %copy.55), calls=%async_computation.3 | async-start | bytes 4194304 | tf_op jit(solution)/shard_map/all_to_all | solution.py:62
  45.6 0.0 all-reduce.3.cloned.1.call-start
  45.6 2.1 convolution_bitcast_fusion.1
  47.7 1.1 convolution_bitcast_fusion.2
  48.8 1.2 convolution_bitcast_fusion
  50.0 0.0 all-reduce.3.cloned.1.call-update
  50.1 0.0 reduce-scatter.2.cloned.1.call-start
  50.2 0.1 all_to_all.65
  50.3 46.2 %all-to-all-done.3 = bf16[12,256,192]{2,0,1:T(8,128)(2,1)} async-done(((bf16[12,256,192]{2,0,1:T(8,128)(2,1)}), bf16[12,256,192]{2,0,1:T(8,128)(2,1)}, u32[]{:S(2)}, u32[]{:S(2)}) %all-to-all-start.3) | async-done | bytes 1179680 | tf_op jit(solution)/shard_map/all_to_all | solution.py:62
  96.5 2.3 copy.57
  98.8 2.8 fusion.11
  101.6 0.0 reduce-scatter.2.cloned.1.call-update
  101.6 0.7 copy-done.7
  102.3 0.8 copy.65
  103.1 4.7 %all-to-all-start = ((s32[12,32,8]{0,2,1:T(8,128)}), s32[12,32,8]{0,2,1:T(8,128)S(1)}, u32[]{:S(2)}, u32[]{:S(2)}) async-start(s32[12,32,8]{0,2,1:T(8,128)} %bitcast), calls=%async_computation | async-start | bytes 262144 | tf_op jit(solution)/shard_map/all_to_all | solution.py:48
  107.7 2.7 copy.50
  110.5 6.5 %all-to-all-done = s32[12,32,8]{0,2,1:T(8,128)S(1)} async-done(((s32[12,32,8]{0,2,1:T(8,128)}), s32[12,32,8]{0,2,1:T(8,128)S(1)}, u32[]{:S(2)}, u32[]{:S(2)}) %all-to-all-start) | async-done | bytes 12320 | tf_op jit(solution)/shard_map/all_to_all | solution.py:48
  117.0 0.1 all_to_all.57
  117.2 0.1 copy.49
  117.3 0.1 reshape.71
  117.4 30.9 %gather_fusion = bf16[3072,192]{1,0:T(8,128)(2,1)} fusion(bf16[8,512,192]{2,1,0:T(8,128)(2,1)S(1)} %copy.50, s32[3072]{0:T(1024)S(1)} %reshape.71), kind=kCustom, calls=%fused_computation | custom fusion | bytes 2383872 | tf_op jit(solution)/shard_map/gather | solution.py:53
  148.3 4.3 %all-to-all-start.1 = ((bf16[384,8,192]{2,1,0:T(8,128)(2,1)}), bf16[384,8,192]{2,1,0:T(8,128)(2,1)S(1)}, u32[]{:S(2)}, u32[]{:S(2)}) async-start(bf16[384,8,192]{2,1,0:T(8,128)(2,1)} %bitcast.83), calls=%async_computation.1 | async-start | bytes 3145728 | tf_op jit(solution)/shard_map/all_to_all | solution.py:54
  152.6 127.6 %psum.31 = f32[192]{0:T(256)S(1)} all-reduce(f32[192]{0:T(256)S(1)} %get-tuple-element.30), channel_id=1, replica_groups=mesh['grp'=16,'emb'=32] {'grp','emb'}, use_global_device_ids=true, to_apply=%region_9.0 | all-reduce | flops 192 | bytes 1536 | tf_op jit(solution)/shard_map/psum | solution.py:67
  280.3 0.6 broadcast_multiply_fusion.6
  280.8 52.6 %all-reduce.3.cloned.1.call-done = (f32[256,128]{0,1:T(8,128)}, f32[128,192]{0,1:T(8,128)}, f32[256,256]{0,1:T(8,128)}) async-done(((f32[256,128]{0,1:T(8,128)}, f32[128,192]{0,1:T(8,128)}, f32[256,256]{0,1:T(8,128)}), (f32[256,128]{0,1:T(8,128)}, f32[128,192]{0,1:T(8,128)}, f32[256,256]{0,1:T(8,128)})) %all-reduce.3.cloned.1.call-update) | async-done | bytes 491536 | tf_op jit(solution)/shard_map/psum | solution.py:67
  333.5 1.0 broadcast_multiply_fusion
  334.5 0.8 copy.62
  335.3 0.9 broadcast_multiply_fusion.1
  336.2 0.8 copy.61
  337.0 0.0 copy-done.6
  337.0 0.7 broadcast_multiply_fusion.2
  337.6 0.0 all-to-all-done.1
  337.6 0.1 copy.71
  337.8 1.5 copy.60
  339.3 1.6 convert_element_type.52
  (10 shorter events, 0.1 us)
Async XLA Ops:
  8.0 15.7 %copy-start = (bf16[256,256]{1,0:T(8,128)(2,1)S(1)}, bf16[256,256]{1,0:T(8,128)(2,1)}, u32[]{:S(2)}) copy-start(bf16[256,256]{1,0:T(8,128)(2,1)} %param.16) | copy-start | bytes 393220
  8.0 15.3 %copy-start.1 = (bf16[12,256,192]{1,2,0:T(8,128)(2,1)S(1)}, bf16[12,256,192]{1,2,0:T(8,128)(2,1)}, u32[]{:S(2)}) copy-start(bf16[12,256,192]{1,2,0:T(8,128)(2,1)} %param.9) | copy-start | bytes 3538948
  9.6 27.6 %all-to-all-start.2 = ((s32[12,32,8]{0,2,1:T(8,128)}), s32[12,32,8]{0,2,1:T(8,128)S(1)}, u32[]{:S(2)}, u32[]{:S(2)}) async-start(s32[12,32,8]{0,2,1:T(8,128)} %bitcast.6), calls=%async_computation.2 | async-start | bytes 262144 | tf_op jit(solution)/shard_map/all_to_all | solution.py:47
  23.7 0.8 copy-start.5
  25.1 1.3 copy-start.3
  25.1 1.3 copy-start.8
  29.5 1.3 copy-start.4
  29.9 0.8 copy-start.2
  37.2 59.3 %all-to-all-start.3 = ((bf16[12,256,192]{2,0,1:T(8,128)(2,1)}), bf16[12,256,192]{2,0,1:T(8,128)(2,1)}, u32[]{:S(2)}, u32[]{:S(2)}) async-start(bf16[12,256,192]{2,0,1:T(8,128)(2,1)} %copy.55), calls=%async_computation.3 | async-start | bytes 4194304 | tf_op jit(solution)/shard_map/all_to_all | solution.py:62
  45.6 287.9 %all-reduce.3.cloned.1.call-start = ((), (), s32[]{:S(2)}) async-start(), calls=%async_computation.6 | async-start | bytes 983040 | tf_op jit(solution)/shard_map/psum | solution.py:67
  50.1 289.2 %reduce-scatter.2.cloned.1.call-start = ((), (), s32[]{:S(2)}) async-start(), calls=%async_computation.5 | async-start | bytes 2228224 | tf_op jit(solution)/shard_map/reduce_scatter | solution.py:64
  101.6 0.7 copy-start.7
  103.1 13.9 %all-to-all-start = ((s32[12,32,8]{0,2,1:T(8,128)}), s32[12,32,8]{0,2,1:T(8,128)S(1)}, u32[]{:S(2)}, u32[]{:S(2)}) async-start(s32[12,32,8]{0,2,1:T(8,128)} %bitcast), calls=%async_computation | async-start | bytes 262144 | tf_op jit(solution)/shard_map/all_to_all | solution.py:48
  148.3 189.3 %all-to-all-start.1 = ((bf16[384,8,192]{2,1,0:T(8,128)(2,1)}), bf16[384,8,192]{2,1,0:T(8,128)(2,1)S(1)}, u32[]{:S(2)}, u32[]{:S(2)}) async-start(bf16[384,8,192]{2,1,0:T(8,128)(2,1)} %bitcast.83), calls=%async_computation.1 | async-start | bytes 3145728 | tf_op jit(solution)/shard_map/all_to_all | solution.py:54
  333.5 3.5 %copy-start.6 = (f32[128,192]{0,1:T(8,128)S(1)}, f32[128,192]{0,1:T(8,128)}, u32[]{:S(2)}) copy-start(f32[128,192]{0,1:T(8,128)} %get-tuple-element.34) | copy-start | bytes 294916
Sparse Core Ops, SparseCore 0:
  52.5 280.9 all-reduce.2
Sparse Core Ops, SparseCore 1:
  101.7 206.0 reduce-scatter.1
where the time goes:
time: 352 us; the launch traced here: 348 us
  blocking collectives  128 us (36%)
  waiting for transfers between devices  105 us (30%)
  local copies, waits for them, and re-layouts  49.2 us (14%)
  starting transfers between devices  29.3 us (8%)
  between operations  15.7 us (4%)
  matrix products  14 us (4%)
  other arithmetic  6.96 us (2%)
    psum x1, blocking collectives, local(): lax.psum((grad_fm, grad_proj, grad_lcb, grad_gain), ('grp', 'emb'))  128 us
    psum x1, waiting for transfers between devices, local(): lax.psum((grad_fm, grad_proj, grad_lcb, grad_gain), ('grp', 'emb'))  52.6 us
    all_to_all x1, waiting for transfers between devices, local(): lax.all_to_all(grad_in, 'emb', split_axis=1, concat_axis=0, tiled=True)  46.2 us
    gather x1, local copies, waits for them, and re-layouts, local(): fetched = tables[feature_pos, next_seen]  30.9 us
    dot_general x13, matrix products, product(): return jnp.einsum(form, left, right, preferred_element_type=jnp.float32)  14 us
    all_to_all x1, starting transfers between devices, local(): lax.all_to_all(ids_now, 'emb', split_axis=1, concat_axis=0, tiled=True)  11.9 us
    unnamed x22, local copies, waits for them, and re-layouts  8.69 us
    all_to_all x1, starting transfers between devices, local(): lax.all_to_all(grad_in, 'emb', split_axis=1, concat_axis=0, tiled=True)  8.34 us
  transfers between devices with their start and end apart: 6, of which 3 were waited for; matrix products, arithmetic and copies ran while one was open for 18% of the time, Pallas kernels for 0%

commit v1 on v0

v1 whole, which is shorter than its diff:
```python
import functools

import jax
import jax.numpy as jnp
from jax import lax
from jax.experimental import pallas as pl
from jax.experimental.pallas import tpu as pltpu
from jax.sharding import PartitionSpec as P

MESH = pl.DeviceIdType.MESH
BF = jnp.bfloat16
F32 = jnp.float32

NE, NG = 32, 16
B, NF, D, K = 12, 256, 192, 128
FL, ROWS = 8, 512
RG = ROWS // NG
J = B // 2
QUADS = 3
QR = 48
CH = QUADS * QR
DT = NE // 8
KK = DT * 128
FP = 4
PR = 3 * RG
NC = NE // 2
HALF = 512
W1 = 8


def nn(a, b):
    return lax.dot_general(a, b, (((1,), (0,)), ((), ())), preferred_element_type=F32)


def nt(a, b):
    return lax.dot_general(a, b, (((1,), (1,)), ((), ())), preferred_element_type=F32)


def iota(shape, axis):
    return lax.broadcasted_iota(jnp.int32, shape, axis)


def loop(lo, hi, body):
    lax.fori_loop(lo, hi, lambda i, c: (body(i), c)[1], 0)


def kernel(
    x_hbm, u_hbm, now_ref, next_ref, tab_hbm, wfm_ref, wproj_ref, wlcb_ref, gain_ref,
    out_next, out_table, out_fm, out_proj, out_lcb, out_gain,
    xb, ub, tab, idt, ids_s, ids_r, now_k, next_k, main_f, tail_f,
    send_n, recv_n, send_d, recv_d, part_s, part_r,
    gfm, gproj, glcb, ggain, wfm_t, wlcb_t,
    dn_s, dn_p, dn_g, dn_c, dn_own, dn_c2, dn_row, dn_g2, dn_full,
    lsem, id_ss, id_rs, n_ss, n_rs, d_ss, d_rs, p_ss, p_rs,
    pr_ss, pr_rs, g1_ss, g1_rs, c1_ss, c1_rs, c2_ss, c2_rs, g2_ss, g2_rs, pl_ss, pl_rs,
):
    g = lax.axis_index("grp")
    e = lax.axis_index("emb")
    core = lax.rem(e, 2)
    chip = e // 2
    mate = e + 1 - 2 * core

    loads = [
        pltpu.make_async_copy(src, dst, lsem.at[i])
        for i, (src, dst) in enumerate(((x_hbm, xb), (u_hbm, ub), (tab_hbm, tab)))
    ]
    for copy in loads:
        copy.start()

    barrier = pltpu.get_barrier_semaphore()

    def greet_emb(k):
        pl.semaphore_signal(barrier, inc=1, device_id=(g, lax.rem(e + k, NE)), device_id_type=MESH)

    def greet_grp(k):
        pl.semaphore_signal(barrier, inc=1, device_id=(lax.rem(g + k, NG), e), device_id_type=MESH)

    loop(1, NE, greet_emb)
    loop(1, NG, greet_grp)

    def emb_copy(src, dst, ss, rs, t, s):
        return pltpu.make_async_remote_copy(
            src_ref=src, dst_ref=dst, send_sem=ss, recv_sem=rs, device_id=(g, t), device_id_type=MESH)

    def grp_copy(src, dst, ss, rs, t):
        return pltpu.make_async_remote_copy(
            src_ref=src, dst_ref=dst, send_sem=ss, recv_sem=rs, device_id=(t, e), device_id_type=MESH)

    idt[...] = jnp.zeros(idt.shape, jnp.int32)
    idt[0:B, :] = next_ref[...]
    idt[16:16 + B, :] = now_ref[...]
    flipped = jnp.transpose(idt[...])
    lane = iota((NF, 128), 1)
    first, second = lane < J, (lane >= 64) & (lane < 64 + J)
    pad = jnp.where((lane < 8) | ((lane >= 64) & (lane < 72)), -1, 0)
    for kind, base in ((0, 0), (1, 16)):
        low = pltpu.roll(flipped, (128 - base) % 128, axis=1) if base else flipped
        high = pltpu.roll(flipped, 64 - J - base, axis=1)
        tile = jnp.where(first, low, jnp.where(second, high, pad))
        ids_s[kind] = tile.reshape(NE, 8, 128)

    wfm_t[...] = jnp.transpose(wfm_ref[...].astype(F32)).astype(BF)
    wlcb_t[...] = jnp.transpose(wlcb_ref[...].astype(F32)).astype(BF)
    gfm[...] = jnp.zeros(gfm.shape, F32)
    gproj[...] = jnp.zeros(gproj.shape, F32)
    glcb[...] = jnp.zeros(glcb.shape, F32)
    ggain[...] = jnp.zeros(ggain.shape, F32)
    for kind in range(2):
        ids_r[kind, e] = ids_s[kind, e]

    pl.semaphore_wait(barrier, NE - 1 + NG - 1)

    def ids_copy(kind, t, s):
        return emb_copy(ids_s.at[kind, t], ids_r.at[kind, s], id_ss.at[kind, t], id_rs.at[kind, s], t, s)

    for kind in range(2):
        loop(1, NE, lambda k: ids_copy(kind, lax.rem(e + k, NE), e).start())

    def n_copy(t, s):
        return emb_copy(send_n.at[t], recv_n.at[s], n_ss.at[t], n_rs.at[s], t, s)

    def d_copy(t, s):
        return emb_copy(send_d.at[t], recv_d.at[s], d_ss.at[t], d_rs.at[s], t, s)

    for copy in loads[:2]:
        copy.wait()

    wfm, wproj, wlcb = wfm_ref[...], wproj_ref[...], wlcb_ref[...]
    gain = gain_ref[...]

    def sample(b):
        x = xb[b]
        xf = x.astype(F32)
        p_t = nn(wfm_t[...], x).astype(BF)
        rows = nt(x, p_t).astype(BF)
        rows_t = nt(p_t, x).astype(BF)
        s = xf + nn(rows, wproj) + nn(wlcb_t[...], x)
        c = s - jnp.sum(s, axis=1, keepdims=True) * (1.0 / D)
        r = lax.rsqrt(jnp.sum(c * c, axis=1, keepdims=True) * (1.0 / D) + 1e-05)
        z = c * r
        up = ub[b].astype(F32)
        ug = up * gain
        m1 = jnp.sum(ug, axis=1, keepdims=True) * (1.0 / D)
        m2 = jnp.sum(ug * z, axis=1, keepdims=True) * (1.0 / D)
        ds = (r * (ug - m1 - z * m2)).astype(BF)
        ggain[...] += jnp.sum((up * z).reshape(NF // 8, 8, D), axis=0)
        dg = nt(ds, wproj).astype(BF)
        dg_t = nt(wproj, ds).astype(BF)
        dp_t = nn(dg_t, x).astype(BF)
        dx = ds.astype(F32) + nn(dg, p_t) + nn(wfm, dp_t) + nn(wlcb, ds)
        gfm[...] += nt(x, dp_t)
        gproj[...] += nn(rows_t, ds)
        glcb[...] += nt(x, ds)
        return dx

    def quad(q):
        mains, tails = [], []
        for i in range(2):
            pair = [sample(2 * q + i), sample(2 * q + i + J)]
            mains += [dx[:, :128].reshape(NE, 8, 128) for dx in pair]
            tails.append(jnp.concatenate([dx[:, 128:] for dx in pair], axis=1).reshape(NE, 8, 128))
        at = pl.multiple_of(q * QR, 16)
        send_d[:, pl.ds(at, 32), :] = jnp.concatenate(mains, axis=1).astype(BF)
        send_d[:, pl.ds(pl.multiple_of(at + 32, 16), 16), :] = jnp.concatenate(tails, axis=1).astype(BF)

    def lookup():
        loop(1, NE, lambda k: ids_copy(0, e, lax.rem(e + NE - k, NE)).wait_recv())
        for dt in range(DT):
            tile = ids_r[0, dt * 8]
            for d8 in range(1, 8):
                tile = tile + pltpu.roll(ids_r[0, dt * 8 + d8], d8 * 8, axis=1)
            next_k[dt * 8:dt * 8 + 8, :] = tile
        next_k[DT * 8:, :] = jnp.zeros((128 - DT * 8, 128), jnp.int32)
        columns = jnp.transpose(next_k[...])
        row = iota((128, ROWS), 1)
        loads[2].wait()
        for f in range(FL):
            hot = jnp.concatenate(
                [(columns[:, dt * 8 + f:dt * 8 + f + 1] == row).astype(F32).astype(BF) for dt in range(DT)], axis=0)
            got = nn(hot, tab[f])
            for dt in range(DT):
                halves = [got[dt * 128 + 64 * p:dt * 128 + 64 * p + 64] for p in range(2)]
                for p in range(2):
                    main_f[pl.ds(dt * 1024 + 8 * p + f, 64, stride=16), :] = halves[p][:, :128]
                tail_f[pl.ds(dt * 512 + f, 64, stride=8), :] = jnp.concatenate([h[:, 128:] for h in halves], axis=1)

        def pack(d):
            for q in range(QUADS):
                m = pl.multiple_of(d * 128 + q * 32, 32)
                t = pl.multiple_of(d * 64 + q * 16, 16)
                send_n[d, q * QR:q * QR + 32, :] = main_f[pl.ds(m, 32), :].astype(BF)
                send_n[d, q * QR + 32:q * QR + 48, :] = tail_f[pl.ds(t, 16), :].astype(BF)

        loop(0, NE, pack)
        recv_n[e] = send_n[e]
        loop(1, W1 + 1, lambda k: n_copy(lax.rem(e + k, NE), e).start())

    def step(q):
        quad(q)

        @pl.when(q == 0)
        def _():
            lookup()

    loop(0, QUADS, step)

    loop(1, NE, lambda k: d_copy(lax.rem(e + k, NE), e).start())
    recv_d[e] = send_d[e]

    dn_s[0:256, :] = gfm[...]
    dn_s[256:512, :] = glcb[:, :128]
    dn_s[512:768, :] = glcb[:, 128:]
    dn_s[768:896, :] = gproj[:, :128]
    tail = gproj[:, 128:]
    dn_s[896:960, :] = jnp.concatenate([tail[:64], tail[64:]], axis=1)
    total = jnp.sum(ggain[...], axis=0, keepdims=True)
    dn_s[960:968, :] = jnp.broadcast_to(total[:, :128], (8, 128))
    dn_s[968:976, :] = jnp.concatenate(
        [jnp.broadcast_to(total[:, 128:], (8, 64)), jnp.zeros((8, 64), F32)], axis=1)
    dn_s[976:1024, :] = jnp.zeros((48, 128), F32)
    theirs = pl.multiple_of((1 - core) * HALF, HALF)
    mine = pl.multiple_of(core * HALF, HALF)
    pair1 = emb_copy(dn_s.at[pl.ds(theirs, HALF)], dn_p, pr_ss, pr_rs, mate, e)
    pair1.start()

    loop(1, NE, lambda k: ids_copy(1, e, lax.rem(e + NE - k, NE)).wait_recv())
    for dt in range(DT):
        tile = ids_r[1, dt * 8]
        for d8 in range(1, 8):
            tile = tile + pltpu.roll(ids_r[1, dt * 8 + d8], d8 * 8, axis=1)
        now_k[:, dt * 128:dt * 128 + 128] = tile

    pair1.wait_recv()
    dn_p[...] += dn_s[pl.ds(mine, HALF), :]

    def g1_copy(t, s):
        return grp_copy(dn_p.at[pl.ds(pl.multiple_of(t * 32, 32), 32)], dn_g.at[s], g1_ss.at[t], g1_rs.at[s], t)

    loop(1, NG, lambda k: g1_copy(lax.rem(g + k, NG), g).start())
    dn_g[g] = dn_p[pl.ds(pl.multiple_of(g * 32, 32), 32), :]

    loop(1, NG, lambda k: g1_copy(g, lax.rem(g + NG - k, NG)).wait_recv())
    dn_c[...] = jnp.sum(dn_g[...], axis=0).reshape(NC, 2, 128)

    def c1_copy(t, s):
        return emb_copy(dn_c.at[t], dn_c2.at[s], c1_ss.at[t], c1_rs.at[s], 2 * t + core, s)

    loop(1, NC, lambda k: c1_copy(lax.rem(chip + k, NC), chip).start())
    dn_c2[chip] = dn_c[chip]

    def unpack(d):
        for q in range(QUADS):
            m = pl.multiple_of(d * 128 + q * 32, 32)
            t = pl.multiple_of(d * 64 + q * 16, 16)
            main_f[pl.ds(m, 32), :] = recv_d[d, q * QR:q * QR + 32, :].astype(F32)
            tail_f[pl.ds(t, 16), :] = recv_d[d, q * QR + 32:q * QR + 48, :].astype(F32)
        main_f[pl.ds(pl.multiple_of(d * 128 + 96, 32), 32), :] = jnp.zeros((32, 128), F32)
        tail_f[pl.ds(pl.multiple_of(d * 64 + 48, 16), 16), :] = jnp.zeros((16, 128), F32)

    def arrive(k):
        s = lax.rem(e + NE - k, NE)
        d_copy(e, s).wait_recv()
        unpack(s)

    unpack(e)
    loop(1, NE, arrive)

    loop(W1 + 1, NE, lambda k: n_copy(lax.rem(e + k, NE), e).start())

    def p_copy(i, t, s):
        rows = pl.ds(pl.multiple_of(i * PR, PR), PR)
        return grp_copy(part_s.at[t, rows], part_r.at[s, rows], p_ss.at[i, t], p_rs.at[i, s], t)

    row_t = iota((ROWS, KK), 0)
    for i in range(FP):
        parts = []
        for f in (2 * i, 2 * i + 1):
            pieces = []
            for dt in range(DT):
                tail = tail_f[pl.ds(dt * 512 + f, 64, stride=8), :]
                for p in range(2):
                    main = main_f[pl.ds(dt * 1024 + 8 * p + f, 64, stride=16), :]
                    pieces.append(jnp.concatenate([main, tail[:, 64 * p:64 * p + 64]], axis=1))
            terms = jnp.concatenate(pieces, axis=0).astype(BF)
            hot = (row_t == now_k[f:f + 1, :]).astype(F32).astype(BF)
            parts.append(nn(hot, terms))
        part_s[:, i * PR:i * PR + RG, :] = parts[0][:, :128].reshape(NG, RG, 128).astype(BF)
        part_s[:, i * PR + RG:i * PR + 2 * RG, :] = parts[1][:, :128].reshape(NG, RG, 128).astype(BF)
        part_s[:, i * PR + 2 * RG:i * PR + 3 * RG, :] = jnp.concatenate(
            [part[:, 128:] for part in parts], axis=1).reshape(NG, RG, 128).astype(BF)
        loop(1, NG, lambda k: p_copy(i, lax.rem(g + k, NG), g).start())
    part_r[g] = part_s[g]

    loop(1, NC, lambda k: c1_copy(chip, lax.rem(chip + NC - k, NC)).wait_recv())
    dn_own[...] = jnp.sum(dn_c2[...], axis=0)

    def c2_copy(t, s):
        return emb_copy(dn_own, dn_row.at[s], c2_ss.at[t], c2_rs.at[s], 2 * t + core, s)

    loop(1, NC, lambda k: c2_copy(lax.rem(chip + k, NC), chip).start())
    dn_row[chip] = dn_own[...]
    loop(1, NC, lambda k: c2_copy(chip, lax.rem(chip + NC - k, NC)).wait_recv())

    def g2_copy(t, s):
        return grp_copy(dn_row, dn_g2.at[s], g2_ss.at[t], g2_rs.at[s], t)

    loop(1, NG, lambda k: g2_copy(lax.rem(g + k, NG), g).start())
    dn_g2[g] = dn_row[...]

    def place(k):
        s0 = pl.multiple_of(2 * k, 2)
        at = pl.multiple_of(16 * k, 16)
        for q in range(QUADS):
            mains = [recv_n[s0 + i, q * QR:q * QR + 32, :].astype(F32).reshape(4, 8, 128) for i in range(2)]
            tails = [recv_n[s0 + i, q * QR + 32:q * QR + 48, :].astype(F32).reshape(2, 8, 128) for i in range(2)]
            main = jnp.concatenate(mains, axis=1)
            tail = jnp.concatenate(tails, axis=1)
            for i in range(2):
                for p in range(2):
                    out_next[2 * q + i + J * p, pl.ds(at, 16), :] = jnp.concatenate(
                        [main[2 * i + p], tail[i, :, 64 * p:64 * p + 64]], axis=1).astype(BF)

    loop(1, NE, lambda k: n_copy(e, lax.rem(e + NE - k, NE)).wait_recv())
    loop(0, NE // 2, place)

    loop(1, NG, lambda k: g2_copy(g, lax.rem(g + NG - k, NG)).wait_recv())

    def half(h, value):
        dn_full[pl.ds(pl.multiple_of(h * HALF, HALF), HALF), :] = value

    half(core, dn_g2[...].reshape(HALF, 128))
    pair2 = emb_copy(
        dn_full.at[pl.ds(mine, HALF)], dn_full.at[pl.ds(mine, HALF)], pl_ss, pl_rs, mate, e)
    pair2.start()

    for i in range(FP):
        loop(1, NG, lambda k: p_copy(i, g, lax.rem(g + NG - k, NG)).wait_recv())
        total = part_r[0, i * PR:(i + 1) * PR, :].astype(F32)
        for s in range(1, NG):
            total = total + part_r[s, i * PR:(i + 1) * PR, :].astype(F32)
        tail = total[2 * RG:]
        out_table[2 * i] = jnp.concatenate([total[:RG], tail[:, :64]], axis=1)
        out_table[2 * i + 1] = jnp.concatenate([total[RG:2 * RG], tail[:, 64:]], axis=1)

    pair2.wait_recv()
    factor = 1.0 / (B * NE * NG)
    out_fm[...] = dn_full[0:256, :] * factor
    out_lcb[:, :128] = dn_full[256:512, :] * factor
    out_lcb[:, 128:] = dn_full[512:768, :] * factor
    tail = dn_full[896:960, :] * factor
    out_proj[...] = jnp.concatenate(
        [dn_full[768:896, :] * factor, jnp.concatenate([tail[:, :64], tail[:, 64:]], axis=0)], axis=1)
    out_gain[...] = jnp.concatenate([dn_full[960:961, :], dn_full[968:969, :64]], axis=1) * factor

    pair1.wait_send()
    pair2.wait_send()

    def drain_emb(k):
        t = lax.rem(e + k, NE)
        for kind in range(2):
            ids_copy(kind, t, e).wait_send()
        n_copy(t, e).wait_send()
        d_copy(t, e).wait_send()

    def drain_chip(k):
        t = lax.rem(chip + k, NC)
        c1_copy(t, chip).wait_send()
        c2_copy(t, chip).wait_send()

    def drain_grp(k):
        t = lax.rem(g + k, NG)
        g1_copy(t, g).wait_send()
        g2_copy(t, g).wait_send()
        for i in range(FP):
            p_copy(i, t, g).wait_send()

    loop(1, NE, drain_emb)
    loop(1, NC, drain_chip)
    loop(1, NG, drain_grp)


def local(pooled, upstream, ids_now, ids_next, tables, w_fm, w_proj, w_lcb, gain):
    vmem = pl.BlockSpec(memory_space=pltpu.VMEM)
    anywhere = pl.BlockSpec(memory_space=pl.ANY)
    dma = pltpu.SemaphoreType.DMA
    scratch = [
        pltpu.VMEM((B, NF, D), BF), pltpu.VMEM((B, NF, D), BF), pltpu.VMEM((FL, ROWS, D), BF),
        pltpu.VMEM((128, NF), jnp.int32), pltpu.VMEM((2, NE, 8, 128), jnp.int32),
        pltpu.VMEM((2, NE, 8, 128), jnp.int32), pltpu.VMEM((8, KK), jnp.int32),
        pltpu.VMEM((128, 128), jnp.int32),
        pltpu.VMEM((NE * 128, 128), F32), pltpu.VMEM((NE * 64, 128), F32),
        pltpu.VMEM((NE, CH, 128), BF), pltpu.VMEM((NE, CH, 128), BF),
        pltpu.VMEM((NE, CH, 128), BF), pltpu.VMEM((NE, CH, 128), BF),
        pltpu.VMEM((NG, FP * PR, 128), BF), pltpu.VMEM((NG, FP * PR, 128), BF),
        pltpu.VMEM((NF, K), F32), pltpu.VMEM((K, D), F32), pltpu.VMEM((NF, NF), F32), pltpu.VMEM((8, D), F32),
        pltpu.VMEM((K, NF), BF), pltpu.VMEM((NF, NF), BF),
        pltpu.VMEM((2 * HALF, 128), F32), pltpu.VMEM((HALF, 128), F32), pltpu.VMEM((NG, 32, 128), F32),
        pltpu.VMEM((NC, 2, 128), F32), pltpu.VMEM((2, 128), F32), pltpu.VMEM((NC, 2, 128), F32),
        pltpu.VMEM((NC, 2, 128), F32), pltpu.VMEM((NG, NC, 2, 128), F32), pltpu.VMEM((2 * HALF, 128), F32),
        dma((3,)), dma((2, NE)), dma((2, NE)), dma((NE,)), dma((NE,)), dma((NE,)), dma((NE,)),
        dma((FP, NG)), dma((FP, NG)), dma, dma, dma((NG,)), dma((NG,)), dma((NC,)), dma((NC,)),
        dma((NC,)), dma((NC,)), dma((NG,)), dma((NG,)), dma, dma,
    ]
    outs = pl.pallas_call(
        kernel,
        out_shape=(
            jax.ShapeDtypeStruct((B, NF, D), BF),
            jax.ShapeDtypeStruct((FL, RG, D), F32),
            jax.ShapeDtypeStruct((NF, K), F32),
            jax.ShapeDtypeStruct((K, D), F32),
            jax.ShapeDtypeStruct((NF, NF), F32),
            jax.ShapeDtypeStruct((1, D), F32),
        ),
        in_specs=[anywhere, anywhere, vmem, vmem, anywhere, vmem, vmem, vmem, vmem],
        out_specs=[vmem] * 6,
        scratch_shapes=scratch,
        compiler_params=pltpu.CompilerParams(
            collective_id=0, has_side_effects=True, vmem_limit_bytes=48 << 20),
        name="layer_and_tables",
    )(pooled, upstream, ids_now, ids_next, tables, w_fm, w_proj, w_lcb, gain.reshape(1, D))
    return outs[:5] + (outs[5].reshape(D),)


def solution(mesh):
    return jax.shard_map(
        local,
        mesh=mesh,
        in_specs=(
            P(("grp", "emb"), None, None),
            P(("grp", "emb"), None, None),
            P(("grp", "emb"), None),
            P(("grp", "emb"), None),
            P("emb", None, None),
            P(),
            P(),
            P(),
            P(),
        ),
        out_specs=(P(("grp", "emb"), None, None), P("emb", "grp", None), P(), P(), P(), P()),
        check_vma=False,
    )
```

time: 352 us -> 135 us (0.38)
  blocking collectives: 128 us -> 0 us
  Pallas kernels: 0 us -> 113 us
  waiting for transfers between devices: 105 us -> 0 us
  local copies, waits for them, and re-layouts: 49.2 us -> 19.9 us
  starting transfers between devices: 29.3 us -> 0 us
  between operations: 15.7 us -> 0.71 us
  matrix products: 14 us -> 0 us
  other arithmetic: 6.96 us -> 0 us
    psum x1 -> x0, blocking collectives: 128 us -> none  [local(): lax.psum((grad_fm, grad_proj, grad_lcb, grad_gain), ('grp', 'emb'))]
    pallas_call x0 -> x1, Pallas kernels: none -> 113 us  [local(): pl.pallas_call(kernel, out_shape=(jax.ShapeDtypeStruct((B, NF, D), BF), j...]
    all_to_all x4 -> x0, waiting for transfers between devices: 52.7 us -> none  [the longest x1 46.2 us: local(): lax.all_to_all(grad_in, 'emb', split_axis=1, concat_axis=0, tiled=True)]
    psum x1 -> x0, waiting for transfers between devices: 52.6 us -> none  [local(): lax.psum((grad_fm, grad_proj, grad_lcb, grad_gain), ('grp', 'emb'))]
    gather x1 -> x0, local copies, waits for them, and re-layouts: 30.9 us -> none  [local(): fetched = tables[feature_pos, next_seen]]
    all_to_all x4 -> x0, starting transfers between devices: 29.3 us -> none  [the longest x1 11.9 us: local(): lax.all_to_all(ids_now, 'emb', split_axis=1, concat_axis=0, tiled=True)]
    dot_general x13 -> x0, matrix products: 14 us -> none  [product(): return jnp.einsum(form, left, right, preferred_element_type=jnp.float32)]
    unnamed x22 -> x38, local copies, waits for them, and re-layouts: 8.69 us -> 19.9 us
  transfers between devices with their start and end apart: 6 -> 0, of which waited for: 3 -> 0; matrix products, arithmetic and copies ran while one was open for 18% -> 0% of each run, Pallas kernels for 0% -> 0%
where the time goes in v1:
time: 135 us; the launch traced here: 133 us
  Pallas kernels  113 us (84%)
  local copies, waits for them, and re-layouts  19.9 us (15%)
    pallas_call x1, Pallas kernels, local(): pl.pallas_call(kernel, out_shape=(jax.ShapeDtypeStruct((B, NF, D), BF), j...  113 us
    unnamed x38, local copies, waits for them, and re-layouts  19.9 us

profile of v1, /device:TPU:6, one launch (start us, length us, event | category | flops | bytes accessed | tf_op | source)
XLA Modules:
  0.0 133.3 jit_solution(5399332303753946972)
XLA Ops:
  0.6 0.9 copy.18.wproj_ref
  1.5 1.6 %copy.15.x_hbm = bf16[12,256,192]{2,1,0:T(8,128)(2,1)S(1)} copy(bf16[12,256,192]{1,2,0:T(8,128)(2,1)} %param.9) | data formatting | bytes 2359296 | tf_op args[0]
  3.2 1.6 %copy.16.u_hbm = bf16[12,256,192]{2,1,0:T(8,128)(2,1)S(1)} copy(bf16[12,256,192]{1,2,0:T(8,128)(2,1)} %param.10) | data formatting | bytes 2359296 | tf_op args[1]
  4.8 0.0 copy-start.8
  4.8 0.0 copy-start.9
  4.8 3.7 %copy.17.tab_hbm = bf16[8,512,192]{2,1,0:T(8,128)(2,1)} copy(bf16[8,512,192]{1,2,0:T(8,128)(2,1)} %param.13) | data formatting | bytes 3145728 | tf_op args[4]
  8.6 0.0 copy-done.8
  8.6 0.0 copy-done.9
  8.6 0.0 copy-start.3
  8.6 0.9 copy-done.3
  9.5 0.0 copy-start.10
  9.5 0.7 copy-done.10
  10.2 0.0 copy-start.11
  10.2 0.7 copy-done.11
  10.9 112.8 %layer_and_tables.1 = (bf16[12,256,192]{2,1,0:T(8,128)(2,1)S(1)}, f32[8,32,192]{2,1,0:T(8,128)S(1)}, f32[256,128]{1,0:T(8,128)S(1)}, f32[128,192]{1,0:T(8,128)S(...) custom-call(bf16[12,256,192]{2,1,0:T(8,128)(2,1)S(1)} %copy.15.x_hbm, bf16[12,256,192]{2,1,0:T(8,128)(2,1)S(1)} %copy.16.u_hbm, ...), custom_call_target="tpu_custom_call" | custom-call | tf_op jit(solution)/shard_map/layer_and_tables/pallas_call | solution.py:404
  123.7 0.0 copy-start
  123.7 1.2 copy-done
  124.8 0.0 copy-start.1
  124.9 0.7 copy-done.1
  125.6 0.0 copy-start.4
  125.6 0.7 copy-done.4
  126.2 0.0 copy-start.6
  126.2 0.7 copy-done.6
  126.9 0.0 copy-start.12
  126.9 0.0 copy-start.5
  126.9 0.0 copy-start.2
  126.9 0.6 copy-done.12
  127.4 0.0 copy-start.7
  127.4 0.0 copy-start.13
  127.4 2.5 %copy.19 = bf16[12,256,192]{1,2,0:T(8,128)(2,1)} copy(bf16[12,256,192]{2,1,0:T(8,128)(2,1)} %copy-done) | data formatting | bytes 2359296
  130.0 0.0 copy-done.5
  130.0 0.7 copy.20
  130.7 0.0 copy-done.2
  130.7 0.7 copy.25
  131.4 0.0 copy-done.7
  131.4 0.7 copy.26
  132.1 0.7 copy.27
  132.8 0.0 copy-done.13
  132.8 0.6 copy.28
Async XLA Ops:
  4.8 3.8 %copy-start.8 = (bf16[256,128]{1,0:T(8,128)(2,1)S(1)}, bf16[256,128]{1,0:T(8,128)(2,1)}, u32[]{:S(2)}) copy-start(bf16[256,128]{1,0:T(8,128)(2,1)} %wfm_ref.1) | copy-start | bytes 196612
  4.8 3.7 %copy-start.9 = (s32[12,256]{1,0:T(8,128)S(1)}, s32[12,256]{1,0:T(8,128)}, u32[]{:S(2)}) copy-start(s32[12,256]{1,0:T(8,128)} %now_ref.1) | copy-start | bytes 36868
  8.6 0.9 copy-start.3
  9.5 0.7 copy-start.10
  10.2 0.7 copy-start.11
  123.7 1.2 copy-start
  124.8 0.7 copy-start.1
  125.6 0.7 copy-start.4
  126.2 0.7 copy-start.6
  126.9 0.6 copy-start.12
  126.9 3.1 %copy-start.5 = (f32[128,192]{1,0:T(8,128)S(1)}, f32[128,192]{1,0:T(8,128)}, u32[]{:S(2)}) copy-start(f32[128,192]{1,0:T(8,128)} %copy-done.4) | copy-start | bytes 294916
  126.9 3.9 %copy-start.2 = (f32[8,32,192]{2,1,0:T(8,128)S(1)}, f32[8,32,192]{2,1,0:T(8,128)}, u32[]{:S(2)}) copy-start(f32[8,32,192]{2,1,0:T(8,128)} %copy-done.1) | copy-start | bytes 589828
  127.4 4.0 %copy-start.7 = (f32[256,128]{1,0:T(8,128)S(1)}, f32[256,128]{1,0:T(8,128)}, u32[]{:S(2)}) copy-start(f32[256,128]{1,0:T(8,128)} %copy-done.6) | copy-start | bytes 393220
  127.4 5.4 %copy-start.13 = (f32[1,192]{1,0:T(1,128)S(1)}, f32[1,192]{1,0:T(1,128)}, u32[]{:S(2)}) copy-start(f32[1,192]{1,0:T(1,128)} %copy-done.12) | copy-start | bytes 2308

commit v2 on v1

v2 whole, which is shorter than its diff:
```python
import functools

import jax
import jax.numpy as jnp
from jax import lax
from jax.experimental import pallas as pl
from jax.experimental.pallas import tpu as pltpu
from jax.sharding import PartitionSpec as P

MESH = pl.DeviceIdType.MESH
BF = jnp.bfloat16
F32 = jnp.float32

NE, NG = 32, 16
B, NF, D, K = 12, 256, 192, 128
FL, ROWS = 8, 512
RG = ROWS // NG
J = B // 2
QUADS = 3
QR = 48
CH = QUADS * QR
DT = NE // 8
KK = DT * 128
FP = 4
NY = NG // 2
PR = 3 * RG
NC = NE // 2
HALF = 512
AHEAD = 0
H1, HOLD = 4, 16


def nn(a, b):
    return lax.dot_general(a, b, (((1,), (0,)), ((), ())), preferred_element_type=F32)


def nt(a, b):
    return lax.dot_general(a, b, (((1,), (1,)), ((), ())), preferred_element_type=F32)


def iota(shape, axis):
    return lax.broadcasted_iota(jnp.int32, shape, axis)


def loop(lo, hi, body):
    lax.fori_loop(lo, hi, lambda i, c: (body(i), c)[1], 0)


def kernel(
    x_hbm, u_hbm, now_hbm, next_hbm, tab_hbm, wfm_hbm, wproj_hbm, wlcb_hbm, gain_hbm,
    recv_n, out_table, dn_full,
    xb, ub, tab, wfm_ref, wproj_t, wlcb_ref, gain_ref,
    next_ref, now_ref, idt, ids_s, ids_r, now_k, next_k, main_f, tail_f,
    send_n, send_d, recv_d, part_s, part_x, part_y, part_r,
    gfm_t, gproj_t, glcb_t, ggain, wfm_t, wproj, gain_c,
    dn_s, dn_p, dn_g, dn_c, dn_own, dn_c2, dn_row, dn_g2,
    lsem, id_ss, id_rs, n_ss, n_rs, d_ss, d_rs, px_ss, px_rs, p_ss, p_rs,
    pr_ss, pr_rs, g1_ss, g1_rs, c1_ss, c1_rs, c2_ss, c2_rs, g2_ss, g2_rs, pl_ss, pl_rs,
):
    g = lax.axis_index("grp")
    e = lax.axis_index("emb")
    core = lax.rem(e, 2)
    chip = e // 2
    mate = e + 1 - 2 * core

    loads = [
        pltpu.make_async_copy(src, dst, lsem.at[i])
        for i, (src, dst) in enumerate((
            (next_hbm, next_ref), (now_hbm, now_ref), (wfm_hbm, wfm_ref),
            (wproj_hbm, wproj_t), (gain_hbm, gain_ref), (x_hbm, xb), (wlcb_hbm, wlcb_ref), (u_hbm, ub),
            (tab_hbm, tab)))
    ]
    for copy in loads:
        copy.start()
    idt[...] = jnp.zeros(idt.shape, jnp.int32)

    barrier = pltpu.get_barrier_semaphore()

    def greet_emb(k):
        pl.semaphore_signal(barrier, inc=1, device_id=(g, lax.rem(e + k, NE)), device_id_type=MESH)

    def greet_grp(k):
        pl.semaphore_signal(barrier, inc=1, device_id=(lax.rem(g + k, NG), e), device_id_type=MESH)

    loop(1, NE, greet_emb)
    loop(1, NG, greet_grp)

    def emb_copy(src, dst, ss, rs, t, s):
        return pltpu.make_async_remote_copy(
            src_ref=src, dst_ref=dst, send_sem=ss, recv_sem=rs, device_id=(g, t), device_id_type=MESH)

    def grp_copy(src, dst, ss, rs, t):
        return pltpu.make_async_remote_copy(
            src_ref=src, dst_ref=dst, send_sem=ss, recv_sem=rs, device_id=(t, e), device_id_type=MESH)

    for copy in loads[:5]:
        copy.wait()
    idt[0:B, :] = next_ref[...]
    idt[16:16 + B, :] = now_ref[...]
    flipped = jnp.transpose(idt[...])
    lane = iota((NF, 128), 1)
    tile = jnp.full((NF, 128), -1, jnp.int32)
    for kind in range(2):
        for p in range(2):
            at = 64 * p + 8 * kind
            moved = flipped if kind + p == 0 else pltpu.roll(flipped, (at - 16 * kind - J * p) % 128, axis=1)
            tile = jnp.where((lane >= at) & (lane < at + J), moved, tile)
    ids_s[...] = tile.reshape(NE, 8, 128)

    wfm_t[...] = jnp.transpose(wfm_ref[...].astype(F32)).astype(BF)
    wproj[...] = jnp.transpose(wproj_t[...].astype(F32)).astype(BF)
    gain_c[...] = jnp.transpose(jnp.broadcast_to(gain_ref[...], (128, D)))
    gfm_t[...] = jnp.zeros(gfm_t.shape, F32)
    gproj_t[...] = jnp.zeros(gproj_t.shape, F32)
    glcb_t[...] = jnp.zeros(glcb_t.shape, F32)
    ggain[...] = jnp.zeros(ggain.shape, F32)
    ids_r[e] = ids_s[e]

    def ids_copy(t, s):
        return emb_copy(ids_s.at[t], ids_r.at[s], id_ss.at[t], id_rs.at[s], t, s)

    def ids_tile(kind, dt):
        lane = lax.rem(iota((8, 128), 1), 64)
        tile = jnp.zeros((8, 128), jnp.int32)
        for d8 in range(8):
            moved = pltpu.roll(ids_r[dt * 8 + d8], (8 * d8 - 8 * kind) % 128, axis=1)
            tile = jnp.where((lane >= 8 * d8) & (lane < 8 * d8 + 8), moved, tile)
        return tile

    def n_copy(t, s):
        return emb_copy(send_n.at[t], recv_n.at[s], n_ss.at[t], n_rs.at[s], t, s)

    def d_copy(q, t, s):
        rows = pl.ds(pl.multiple_of(q * QR, QR), QR)
        return emb_copy(send_d.at[t, rows], recv_d.at[s, rows], d_ss.at[q, t], d_rs.at[q, s], t, s)

    for copy in loads[5:8]:
        copy.wait()

    def sample(b):
        x = xb[b]
        p_t = nt(wfm_t[...], x).astype(BF)
        rows_t = nn(p_t, x).astype(BF)
        s = x.astype(F32) + nn(wproj_t[...], rows_t) + nn(x, wlcb_ref[...])
        c = s - jnp.sum(s, axis=0, keepdims=True) * (1.0 / D)
        r = lax.rsqrt(jnp.sum(c * c, axis=0, keepdims=True) * (1.0 / D) + 1e-05)
        z = c * r
        up = ub[b].astype(F32)
        gain = gain_c[...]
        ug = up * jnp.concatenate([gain, gain], axis=1)
        m1 = jnp.sum(ug, axis=0, keepdims=True) * (1.0 / D)
        m2 = jnp.sum(ug * z, axis=0, keepdims=True) * (1.0 / D)
        ds_t = (r * (ug - m1 - z * m2)).astype(BF)
        uz = up * z
        ggain[...] += uz[:, :128] + uz[:, 128:]
        ds_f = jnp.transpose(ds_t.astype(F32))
        ds = ds_f.astype(BF)
        dg_t = nn(wproj[...], ds_t).astype(BF)
        dg = nt(ds, wproj[...]).astype(BF)
        dp_t = nt(dg_t, x).astype(BF)
        dx = ds_f + nn(wlcb_ref[...], ds) + nn(
            jnp.concatenate([dg, wfm_ref[...]], axis=1), jnp.concatenate([p_t, dp_t], axis=0))
        gfm_t[...] += nn(dp_t, x)
        gproj_t[...] += nt(ds_t, rows_t)
        glcb_t[...] += nn(ds, x)
        return dx

    def quad(q):
        mains, tails = [], []
        for i in range(2):
            pair = [sample(2 * q + i), sample(2 * q + i + J)]
            mains += [dx[:, :128].reshape(NE, 8, 128) for dx in pair]
            tails.append(jnp.concatenate([dx[:, 128:] for dx in pair], axis=1).reshape(NE, 8, 128))
        at = pl.multiple_of(q * QR, 16)
        send_d[:, pl.ds(at, 32), :] = jnp.concatenate(mains, axis=1).astype(BF)
        send_d[:, pl.ds(pl.multiple_of(at + 32, 16), 16), :] = jnp.concatenate(tails, axis=1).astype(BF)

    def lookup():
        loop(1, NE, lambda k: ids_copy(e, lax.rem(e + NE - k, NE)).wait_recv())
        for dt in range(DT):
            next_k[dt * 8:dt * 8 + 8, :] = ids_tile(0, dt)
            now_k[:, dt * 128:dt * 128 + 128] = ids_tile(1, dt)
        next_k[DT * 8:, :] = jnp.zeros((128 - DT * 8, 128), jnp.int32)
        columns = jnp.transpose(next_k[...])
        row = iota((128, ROWS), 1)
        loads[8].wait()
        for f in range(FL):
            hot = jnp.concatenate(
                [(columns[:, dt * 8 + f:dt * 8 + f + 1] == row).astype(F32).astype(BF) for dt in range(DT)], axis=0)
            got = nt(hot, tab[f])
            for dt in range(DT):
                halves = [got[dt * 128 + 64 * p:dt * 128 + 64 * p + 64] for p in range(2)]
                for p in range(2):
                    main_f[pl.ds(dt * 1024 + 8 * p + f, 64, stride=16), :] = halves[p][:, :128]
                tail_f[pl.ds(dt * 512 + f, 64, stride=8), :] = jnp.concatenate([h[:, 128:] for h in halves], axis=1)

        def pack(d):
            for q in range(QUADS):
                m = pl.multiple_of(d * 128 + q * 32, 32)
                t = pl.multiple_of(d * 64 + q * 16, 16)
                send_n[d, q * QR:q * QR + 32, :] = main_f[pl.ds(m, 32), :].astype(BF)
                send_n[d, q * QR + 32:q * QR + 48, :] = tail_f[pl.ds(t, 16), :].astype(BF)

        loop(0, NE, pack)
        recv_n[e] = send_n[e]

    def send_quad(q):
        loop(1, NE, lambda k: d_copy(q, lax.rem(e + k, NE), e).start())

    def enter():
        pl.semaphore_wait(barrier, NE - 1 + NG - 1)
        loop(1, NE, lambda k: ids_copy(lax.rem(e + k, NE), e).start())

    if AHEAD == 0:
        enter()

    def step(q):
        quad(q)

        @pl.when(q == AHEAD - 1)
        def _():
            enter()
            for before in range(AHEAD - 1):
                send_quad(before)

        @pl.when(q >= AHEAD - 1)
        def _():
            send_quad(q)

    loop(0, QUADS, step)
    recv_d[e] = send_d[e]

    for h in range(2):
        dn_s[128 * h:128 * h + 128, :] = gfm_t[:, 128 * h:128 * h + 128]
        dn_s[256 + 256 * h:512 + 256 * h, :] = glcb_t[:, 128 * h:128 * h + 128]
    dn_s[768:960, :] = gproj_t[...]
    total = jnp.sum(jnp.transpose(ggain[...]), axis=0, keepdims=True)
    dn_s[960:968, :] = jnp.broadcast_to(total[:, :128], (8, 128))
    dn_s[968:976, :] = jnp.concatenate(
        [jnp.broadcast_to(total[:, 128:], (8, 64)), jnp.zeros((8, 64), F32)], axis=1)
    dn_s[976:1024, :] = jnp.zeros((48, 128), F32)
    theirs = pl.multiple_of((1 - core) * HALF, HALF)
    mine = pl.multiple_of(core * HALF, HALF)
    pair1 = emb_copy(dn_s.at[pl.ds(theirs, HALF)], dn_p, pr_ss, pr_rs, mate, e)
    pair1.start()

    lookup()

    pair1.wait_recv()
    dn_p[...] += dn_s[pl.ds(mine, HALF), :]

    def g1_copy(t, s):
        return grp_copy(dn_p.at[pl.ds(pl.multiple_of(t * 32, 32), 32)], dn_g.at[s], g1_ss.at[t], g1_rs.at[s], t)

    loop(1, NG, lambda k: g1_copy(lax.rem(g + k, NG), g).start())
    dn_g[g] = dn_p[pl.ds(pl.multiple_of(g * 32, 32), 32), :]

    def unpack(d):
        for q in range(QUADS):
            m = pl.multiple_of(d * 128 + q * 32, 32)
            t = pl.multiple_of(d * 64 + q * 16, 16)
            main_f[pl.ds(m, 32), :] = recv_d[d, q * QR:q * QR + 32, :].astype(F32)
            tail_f[pl.ds(t, 16), :] = recv_d[d, q * QR + 32:q * QR + 48, :].astype(F32)
        main_f[pl.ds(pl.multiple_of(d * 128 + 96, 32), 32), :] = jnp.zeros((32, 128), F32)
        tail_f[pl.ds(pl.multiple_of(d * 64 + 48, 16), 16), :] = jnp.zeros((16, 128), F32)

    def arrive(k):
        s = lax.rem(e + NE - k, NE)
        for q in range(QUADS):
            d_copy(q, e, s).wait_recv()
        unpack(s)

    def arrive_send(k):
        arrive(k)
        n_copy(lax.rem(e + k - HOLD + 1, NE), e).start()

    unpack(e)
    loop(1, H1, arrive)

    loop(1, NG, lambda k: g1_copy(g, lax.rem(g + NG - k, NG)).wait_recv())
    dn_c[...] = jnp.sum(dn_g[...], axis=0).reshape(NC, 2, 128)

    def c1_copy(t, s):
        return emb_copy(dn_c.at[t], dn_c2.at[s], c1_ss.at[t], c1_rs.at[s], 2 * t + core, s)

    loop(1, NC, lambda k: c1_copy(lax.rem(chip + k, NC), chip).start())
    dn_c2[chip] = dn_c[chip]

    loop(H1, HOLD, arrive)

    loop(1, NC, lambda k: c1_copy(chip, lax.rem(chip + NC - k, NC)).wait_recv())
    dn_own[...] = jnp.sum(dn_c2[...], axis=0)

    def c2_copy(t, s):
        return emb_copy(dn_own, dn_row.at[s], c2_ss.at[t], c2_rs.at[s], 2 * t + core, s)

    loop(1, NC, lambda k: c2_copy(lax.rem(chip + k, NC), chip).start())
    dn_row[chip] = dn_own[...]
    loop(HOLD, NE, arrive_send)
    loop(NE - HOLD + 1, NE, lambda k: n_copy(lax.rem(e + k, NE), e).start())

    y, xh = g // 2, lax.rem(g, 2)

    def px_copy(i):
        rows = pl.ds(i * PR, PR)
        return pltpu.make_async_remote_copy(
            src_ref=part_s.at[1 - xh, :, rows], dst_ref=part_x.at[:, rows], send_sem=px_ss.at[i],
            recv_sem=px_rs.at[i], device_id=(2 * y + 1 - xh, e), device_id_type=MESH)

    def p_copy(i, t, s):
        rows = pl.ds(pl.multiple_of(i * PR, PR), PR)
        return grp_copy(part_y.at[t, rows], part_r.at[s, rows], p_ss.at[i, t], p_rs.at[i, s], 2 * t + xh)

    row_t = iota((ROWS, KK), 0)
    for i in range(FP):
        parts = []
        for f in (2 * i, 2 * i + 1):
            pieces = []
            for dt in range(DT):
                tail = tail_f[pl.ds(dt * 512 + f, 64, stride=8), :]
                for p in range(2):
                    main = main_f[pl.ds(dt * 1024 + 8 * p + f, 64, stride=16), :]
                    pieces.append(jnp.concatenate([main, tail[:, 64 * p:64 * p + 64]], axis=1))
            terms = jnp.concatenate(pieces, axis=0).astype(BF)
            hot = (row_t == now_k[f:f + 1, :]).astype(F32).astype(BF)
            parts.append(nn(hot, terms))
        mains = [part[:, :128].reshape(NY, 2, RG, 128) for part in parts]
        tail = jnp.concatenate([part[:, 128:] for part in parts], axis=1).reshape(NY, 2, RG, 128)
        for h in range(2):
            part_s[h, :, i * PR:(i + 1) * PR, :] = jnp.concatenate(
                [mains[0][:, h], mains[1][:, h], tail[:, h]], axis=1).astype(BF)
        px_copy(i).start()

    loop(1, NC, lambda k: c2_copy(chip, lax.rem(chip + NC - k, NC)).wait_recv())

    def g2_copy(t, s):
        return grp_copy(dn_row, dn_g2.at[s], g2_ss.at[t], g2_rs.at[s], t)

    loop(1, NG, lambda k: g2_copy(lax.rem(g + k, NG), g).start())
    dn_g2[g] = dn_row[...]

    for i in range(FP):
        rows = slice(i * PR, (i + 1) * PR)
        px_copy(i).wait_recv()
        part_y[:, rows, :] = (part_s[xh, :, rows, :].astype(F32) + part_x[:, rows, :].astype(F32)).astype(BF)
        loop(1, NY, lambda k: p_copy(i, lax.rem(y + k, NY), y).start())
    part_r[y] = part_y[y]

    loop(1, NG, lambda k: g2_copy(g, lax.rem(g + NG - k, NG)).wait_recv())

    def half(h, value):
        dn_full[pl.ds(pl.multiple_of(h * HALF, HALF), HALF), :] = value

    half(core, dn_g2[...].reshape(HALF, 128))
    pair2 = emb_copy(
        dn_full.at[pl.ds(mine, HALF)], dn_full.at[pl.ds(mine, HALF)], pl_ss, pl_rs, mate, e)
    pair2.start()

    loop(1, NE, lambda k: n_copy(e, lax.rem(e + NE - k, NE)).wait_recv())

    for i in range(FP):
        loop(1, NY, lambda k: p_copy(i, y, lax.rem(y + NY - k, NY)).wait_recv())
        total = part_r[0, i * PR:(i + 1) * PR, :].astype(F32)
        for s in range(1, NY):
            total = total + part_r[s, i * PR:(i + 1) * PR, :].astype(F32)
        tail = total[2 * RG:]
        out_table[2 * i] = jnp.concatenate([total[:RG], tail[:, :64]], axis=1)
        out_table[2 * i + 1] = jnp.concatenate([total[RG:2 * RG], tail[:, 64:]], axis=1)

    pair2.wait_recv()

    pair1.wait_send()
    pair2.wait_send()

    def drain_emb(k):
        t = lax.rem(e + k, NE)
        ids_copy(t, e).wait_send()
        n_copy(t, e).wait_send()
        for q in range(QUADS):
            d_copy(q, t, e).wait_send()

    def drain_chip(k):
        t = lax.rem(chip + k, NC)
        c1_copy(t, chip).wait_send()
        c2_copy(t, chip).wait_send()

    def drain_grp(k):
        t = lax.rem(g + k, NG)
        g1_copy(t, g).wait_send()
        g2_copy(t, g).wait_send()

    loop(1, NE, drain_emb)
    loop(1, NC, drain_chip)
    loop(1, NG, drain_grp)
    for i in range(FP):
        px_copy(i).wait_send()
        loop(1, NY, lambda k: p_copy(i, lax.rem(y + k, NY), y).wait_send())


def finish(recv_n, table, dense, out_next, out_table, out_fm, out_proj, out_lcb, out_gain):
    @pl.when(pl.program_id(0) == 0)
    def _():
        out_table[...] = table[...]
        factor = 1.0 / (B * NE * NG)
        for h in range(2):
            rows = pl.ds(128 * h, 128)
            out_fm[rows, :] = jnp.transpose(dense[128 * h:128 * h + 128, :] * factor)
            for w in range(2):
                out_lcb[rows, 128 * w:128 * w + 128] = jnp.transpose(
                    dense[256 + 256 * h + 128 * w:384 + 256 * h + 128 * w, :] * factor)
        out_proj[...] = dense[768:960, :] * factor
        out_gain[...] = jnp.concatenate([dense[960:961, :], dense[968:969, :64]], axis=1) * factor

    tail = recv_n[:, 32:48, :].astype(F32)
    for i in range(2):
        main = recv_n[:, 16 * i:16 * i + 16, :].astype(F32)
        tails = jnp.transpose(tail[:, 8 * i:8 * i + 8].reshape(NF, 128)).astype(BF)
        for p in range(2):
            out_next[p, i, 0:128, :] = jnp.transpose(main[:, 8 * p:8 * p + 8].reshape(NF, 128)).astype(BF)
            out_next[p, i, 128:192, :] = tails[64 * p:64 * p + 64]


def whole(*shape):
    return pl.BlockSpec(shape, lambda q: (0,) * len(shape))


def local(pooled, upstream, ids_now, ids_next, tables, w_fm, w_proj, w_lcb, gain):
    vmem = pl.BlockSpec(memory_space=pltpu.VMEM)
    anywhere = pl.BlockSpec(memory_space=pltpu.HBM)
    dma = pltpu.SemaphoreType.DMA
    scratch = [
        pltpu.VMEM((B, D, NF), BF), pltpu.VMEM((B, D, NF), BF), pltpu.VMEM((FL, D, ROWS), BF),
        pltpu.VMEM((NF, K), BF), pltpu.VMEM((D, K), BF), pltpu.VMEM((NF, NF), BF), pltpu.VMEM((1, D), F32),
        pltpu.VMEM((B, NF), jnp.int32), pltpu.VMEM((B, NF), jnp.int32), pltpu.VMEM((128, NF), jnp.int32),
        pltpu.VMEM((NE, 8, 128), jnp.int32),
        pltpu.VMEM((NE, 8, 128), jnp.int32), pltpu.VMEM((8, KK), jnp.int32),
        pltpu.VMEM((128, 128), jnp.int32),
        pltpu.VMEM((NE * 128, 128), F32), pltpu.VMEM((NE * 64, 128), F32),
        pltpu.VMEM((NE, CH, 128), BF),
        pltpu.VMEM((NE, CH, 128), BF), pltpu.VMEM((NE, CH, 128), BF),
        pltpu.VMEM((2, NY, FP * PR, 128), BF), pltpu.VMEM((NY, FP * PR, 128), BF),
        pltpu.VMEM((NY, FP * PR, 128), BF), pltpu.VMEM((NY, FP * PR, 128), BF),
        pltpu.VMEM((K, NF), F32), pltpu.VMEM((D, K), F32), pltpu.VMEM((NF, NF), F32), pltpu.VMEM((D, 128), F32),
        pltpu.VMEM((K, NF), BF), pltpu.VMEM((K, D), BF), pltpu.VMEM((D, 128), F32),
        pltpu.VMEM((2 * HALF, 128), F32), pltpu.VMEM((HALF, 128), F32), pltpu.VMEM((NG, 32, 128), F32),
        pltpu.VMEM((NC, 2, 128), F32), pltpu.VMEM((2, 128), F32), pltpu.VMEM((NC, 2, 128), F32),
        pltpu.VMEM((NC, 2, 128), F32), pltpu.VMEM((NG, NC, 2, 128), F32),
        dma((9,)), dma((NE,)), dma((NE,)), dma((NE,)), dma((NE,)), dma((QUADS, NE)), dma((QUADS, NE)),
        dma((FP,)), dma((FP,)), dma((FP, NY)), dma((FP, NY)), dma, dma, dma((NG,)), dma((NG,)), dma((NC,)), dma((NC,)),
        dma((NC,)), dma((NC,)), dma((NG,)), dma((NG,)), dma, dma,
    ]
    held = pl.pallas_call(
        kernel,
        out_shape=(
            jax.ShapeDtypeStruct((NE, CH, 128), BF),
            jax.ShapeDtypeStruct((FL, RG, D), F32),
            jax.ShapeDtypeStruct((2 * HALF, 128), F32),
        ),
        in_specs=[anywhere] * 9,
        out_specs=[vmem] * 3,
        scratch_shapes=scratch,
        compiler_params=pltpu.CompilerParams(
            collective_id=0, has_side_effects=True, vmem_limit_bytes=62 << 20),
        name="layer_and_tables",
    )(
        jnp.swapaxes(pooled, 1, 2), jnp.swapaxes(upstream, 1, 2), ids_now, ids_next,
        jnp.swapaxes(tables, 1, 2), w_fm, w_proj.T, w_lcb, gain.reshape(1, D))
    outs = pl.pallas_call(
        finish,
        out_shape=(
            jax.ShapeDtypeStruct((2, J, D, NF), BF),
            jax.ShapeDtypeStruct((FL, RG, D), F32),
            jax.ShapeDtypeStruct((NF, K), F32),
            jax.ShapeDtypeStruct((D, K), F32),
            jax.ShapeDtypeStruct((NF, NF), F32),
            jax.ShapeDtypeStruct((1, D), F32),
        ),
        grid=(QUADS,),
        in_specs=[pl.BlockSpec((NE, QR, 128), lambda q: (0, q, 0)), whole(FL, RG, D), whole(2 * HALF, 128)],
        out_specs=[
            pl.BlockSpec((2, 2, D, NF), lambda q: (0, q, 0, 0)), whole(FL, RG, D), whole(NF, K), whole(D, K),
            whole(NF, NF), whole(1, D)],
        compiler_params=pltpu.CompilerParams(vmem_limit_bytes=62 << 20),
        name="finish",
    )(*held)
    return (
        jnp.swapaxes(outs[0].reshape(B, D, NF), 1, 2), outs[1], outs[2], outs[3].T, outs[4], outs[5].reshape(D))


def solution(mesh):
    return jax.shard_map(
        local,
        mesh=mesh,
        in_specs=(
            P(("grp", "emb"), None, None),
            P(("grp", "emb"), None, None),
            P(("grp", "emb"), None),
            P(("grp", "emb"), None),
            P("emb", None, None),
            P(),
            P(),
            P(),
            P(),
        ),
        out_specs=(P(("grp", "emb"), None, None), P("emb", "grp", None), P(), P(), P(), P()),
        check_vma=False,
    )
```

time: 135 us -> 103 us (0.76)
  local copies, waits for them, and re-layouts: 19.9 us -> 0 us
  Pallas kernels: 113 us -> 101 us
    unnamed x38 -> x0, local copies, waits for them, and re-layouts: 19.9 us -> none
    pallas_call x1 -> x2, Pallas kernels: 113 us -> 101 us  [the longest x1 96.9 us: local(): pl.pallas_call(kernel, out_shape=(jax.ShapeDtypeStruct((NE, CH, 128), BF)...]
where the time goes in v2:
time: 103 us; the launch traced here: 102 us
  Pallas kernels  101 us (98%)
    pallas_call x1, Pallas kernels, local(): pl.pallas_call(kernel, out_shape=(jax.ShapeDtypeStruct((NE, CH, 128), BF)...  96.9 us
    pallas_call x1, Pallas kernels, local(): pl.pallas_call(finish, out_shape=(jax.ShapeDtypeStruct((2, J, D, NF), BF)...  4.06 us

profile of v2, /device:TPU:6, one launch (start us, length us, event | category | flops | bytes accessed | tf_op | source)
XLA Modules:
  0.0 101.6 jit_solution(6361815674943513413)
XLA Ops:
  0.6 96.9 %layer_and_tables.1 = (bf16[32,144,128]{2,1,0:T(8,128)(2,1)}, f32[8,32,192]{2,1,0:T(8,128)}, f32[1024,128]{1,0:T(8,128)}) custom-call(bf16[12,192,256]{2,1,0:T(8,128)(2,1)} %bitcast.11, bf16[12,192,256]{2,1,0:T(8,128)(2,1)} %bitcast.12, s32[12,256]{1,0:T(8,128)} %now_hbm.1, s32[12,256]{1,0:T(8,128)} %next_hbm.1, bf16[8,192,512]{2,1,0:T(8,128)(2,1)} %bitcast.10, ...), custom_call_target="tpu_custom_call" | custom-call | tf_op jit(solution)/shard_map/layer_and_tables/pallas_call | solution.py:452
  97.6 4.1 %finish.1 = (bf16[2,6,192,256]{3,2,1,0:T(8,128)(2,1)}, f32[8,32,192]{2,1,0:T(8,128)}, f32[256,128]{1,0:T(8,128)}, f32[192,128]{1,0:T(8,128)}, f32[256,256]{1,0:T(8,128)}, /*index=5*/f32[1,192]{1,0:T(1,128)}) custom-call(bf16[32,144,128]{2,1,0:T(8,128)(2,1)} %get-tuple-element.15.recv_n, f32[8,32,192]{2,1,0:T(8,128)} %get-tuple-element.16.table, ...), custom_call_target="tpu_custom_call" | custom-call | tf_op jit(solution)/shard_map/finish/pallas_call | solution.py:468

commit v3 on v2

--- a/solution.py
+++ b/solution.py
@@ -1,5 +1,3 @@
-import functools
-
 import jax
 import jax.numpy as jnp
 from jax import lax
@@ -23,11 +21,12 @@
 KK = DT * 128
 FP = 4
 NY = NG // 2
+YF = 2
 PR = 3 * RG
 NC = NE // 2
 HALF = 512
 AHEAD = 0
-H1, HOLD = 4, 16
+H1, HOLD = 4, 17
 
 
 def nn(a, b):
@@ -51,10 +50,10 @@
     recv_n, out_table, dn_full,
     xb, ub, tab, wfm_ref, wproj_t, wlcb_ref, gain_ref,
     next_ref, now_ref, idt, ids_s, ids_r, now_k, next_k, main_f, tail_f,
-    send_n, send_d, recv_d, part_s, part_x, part_y, part_r,
+    send_n, send_d, recv_d, part_s, part_x, part_y, part_r, part_z, part_t, part_w, part_v,
     gfm_t, gproj_t, glcb_t, ggain, wfm_t, wproj, gain_c,
     dn_s, dn_p, dn_g, dn_c, dn_own, dn_c2, dn_row, dn_g2,
-    lsem, id_ss, id_rs, n_ss, n_rs, d_ss, d_rs, px_ss, px_rs, p_ss, p_rs,
+    lsem, id_ss, id_rs, n_ss, n_rs, d_ss, d_rs, px_ss, px_rs, p_ss, p_rs, z_ss, z_rs, w_ss, w_rs,
     pr_ss, pr_rs, g1_ss, g1_rs, c1_ss, c1_rs, c2_ss, c2_rs, g2_ss, g2_rs, pl_ss, pl_rs,
 ):
     g = lax.axis_index("grp")
@@ -270,9 +269,16 @@
             d_copy(q, e, s).wait_recv()
         unpack(s)
 
+    zc, xl = e // 4, lax.rem(chip, 2)
+
+    def n_send(i):
+        r = lax.rem(i, NC)
+        t = lax.rem(zc + r // 2, NE // 4) * 4 + lax.rem(xl + i // NC, 2) * 2 + lax.rem(core + r, 2)
+        n_copy(t, e).start()
+
     def arrive_send(k):
         arrive(k)
-        n_copy(lax.rem(e + k - HOLD + 1, NE), e).start()
+        n_send(k - HOLD + 1)
 
     unpack(e)
     loop(1, H1, arrive)
@@ -297,7 +303,7 @@
     loop(1, NC, lambda k: c2_copy(lax.rem(chip + k, NC), chip).start())
     dn_row[chip] = dn_own[...]
     loop(HOLD, NE, arrive_send)
-    loop(NE - HOLD + 1, NE, lambda k: n_copy(lax.rem(e + k, NE), e).start())
+    loop(NE - HOLD + 1, NC, n_send)
 
     y, xh = g // 2, lax.rem(g, 2)
 
@@ -310,6 +316,17 @@
     def p_copy(i, t, s):
         rows = pl.ds(pl.multiple_of(i * PR, PR), PR)
         return grp_copy(part_y.at[t, rows], part_r.at[s, rows], p_ss.at[i, t], p_rs.at[i, s], 2 * t + xh)
+
+    def z_copy(i, t, s):
+        rows = pl.ds(i * PR, PR)
+        return grp_copy(
+            part_s.at[:, t, rows], part_z.at[s, :, rows], z_ss.at[i, t], z_rs.at[i, s], 2 * t + xh)
+
+    def w_copy(i):
+        rows = pl.ds(i * PR, PR)
+        return pltpu.make_async_remote_copy(
+            src_ref=part_w.at[rows], dst_ref=part_v.at[rows], send_sem=w_ss.at[i], recv_sem=w_rs.at[i],
+            device_id=(2 * y + 1 - xh, e), device_id_type=MESH)
 
     row_t = iota((ROWS, KK), 0)
     for i in range(FP):
@@ -329,7 +346,11 @@
         for h in range(2):
             part_s[h, :, i * PR:(i + 1) * PR, :] = jnp.concatenate(
                 [mains[0][:, h], mains[1][:, h], tail[:, h]], axis=1).astype(BF)
-        px_copy(i).start()
+        if i < YF:
+            loop(1, NY, lambda k: z_copy(i, lax.rem(y + k, NY), y).start())
+            part_z[y, :, i * PR:(i + 1) * PR, :] = part_s[:, y, i * PR:(i + 1) * PR, :]
+        else:
+            px_copy(i).start()
 
     loop(1, NC, lambda k: c2_copy(chip, lax.rem(chip + NC - k, NC)).wait_recv())
 
@@ -339,12 +360,23 @@
     loop(1, NG, lambda k: g2_copy(lax.rem(g + k, NG), g).start())
     dn_g2[g] = dn_row[...]
 
-    for i in range(FP):
+    for i in range(YF, FP):
         rows = slice(i * PR, (i + 1) * PR)
         px_copy(i).wait_recv()
         part_y[:, rows, :] = (part_s[xh, :, rows, :].astype(F32) + part_x[:, rows, :].astype(F32)).astype(BF)
         loop(1, NY, lambda k: p_copy(i, lax.rem(y + k, NY), y).start())
-    part_r[y] = part_y[y]
+    loop(NC, NE, n_send)
+    part_r[y, YF * PR:, :] = part_y[y, YF * PR:, :]
+
+    for i in range(YF):
+        rows = slice(i * PR, (i + 1) * PR)
+        loop(1, NY, lambda k: z_copy(i, y, lax.rem(y + NY - k, NY)).wait_recv())
+        total = part_z[0, :, rows, :].astype(F32)
+        for s in range(1, NY):
+            total = total + part_z[s, :, rows, :].astype(F32)
+        part_t[:, rows, :] = total
+        part_w[rows, :] = part_t[1 - xh, rows, :].astype(BF)
+        w_copy(i).start()
 
     loop(1, NG, lambda k: g2_copy(g, lax.rem(g + NG - k, NG)).wait_recv())
 
@@ -356,16 +388,21 @@
         dn_full.at[pl.ds(mine, HALF)], dn_full.at[pl.ds(mine, HALF)], pl_ss, pl_rs, mate, e)
     pair2.start()
 
-    loop(1, NE, lambda k: n_copy(e, lax.rem(e + NE - k, NE)).wait_recv())
-
     for i in range(FP):
-        loop(1, NY, lambda k: p_copy(i, y, lax.rem(y + NY - k, NY)).wait_recv())
-        total = part_r[0, i * PR:(i + 1) * PR, :].astype(F32)
-        for s in range(1, NY):
-            total = total + part_r[s, i * PR:(i + 1) * PR, :].astype(F32)
+        rows = slice(i * PR, (i + 1) * PR)
+        if i < YF:
+            w_copy(i).wait_recv()
+            total = part_t[xh, rows, :] + part_v[rows, :].astype(F32)
+        else:
+            loop(1, NY, lambda k: p_copy(i, y, lax.rem(y + NY - k, NY)).wait_recv())
+            total = part_r[0, rows, :].astype(F32)
+            for s in range(1, NY):
+                total = total + part_r[s, rows, :].astype(F32)
         tail = total[2 * RG:]
         out_table[2 * i] = jnp.concatenate([total[:RG], tail[:, :64]], axis=1)
         out_table[2 * i + 1] = jnp.concatenate([total[RG:2 * RG], tail[:, 64:]], axis=1)
+
+    loop(1, NE, lambda k: n_copy(e, lax.rem(e + NE - k, NE)).wait_recv())
 
     pair2.wait_recv()
 
@@ -393,8 +430,12 @@
     loop(1, NC, drain_chip)
     loop(1, NG, drain_grp)
     for i in range(FP):
-        px_copy(i).wait_send()
-        loop(1, NY, lambda k: p_copy(i, lax.rem(y + k, NY), y).wait_send())
+        if i < YF:
+            loop(1, NY, lambda k: z_copy(i, lax.rem(y + k, NY), y).wait_send())
+            w_copy(i).wait_send()
+        else:
+            px_copy(i).wait_send()
+            loop(1, NY, lambda k: p_copy(i, lax.rem(y + k, NY), y).wait_send())
 
 
 def finish(recv_n, table, dense, out_next, out_table, out_fm, out_proj, out_lcb, out_gain):
@@ -440,13 +481,16 @@
         pltpu.VMEM((NE, CH, 128), BF), pltpu.VMEM((NE, CH, 128), BF),
         pltpu.VMEM((2, NY, FP * PR, 128), BF), pltpu.VMEM((NY, FP * PR, 128), BF),
         pltpu.VMEM((NY, FP * PR, 128), BF), pltpu.VMEM((NY, FP * PR, 128), BF),
+        pltpu.VMEM((NY, 2, YF * PR, 128), BF), pltpu.VMEM((2, YF * PR, 128), F32),
+        pltpu.VMEM((YF * PR, 128), BF), pltpu.VMEM((YF * PR, 128), BF),
         pltpu.VMEM((K, NF), F32), pltpu.VMEM((D, K), F32), pltpu.VMEM((NF, NF), F32), pltpu.VMEM((D, 128), F32),
         pltpu.VMEM((K, NF), BF), pltpu.VMEM((K, D), BF), pltpu.VMEM((D, 128), F32),
         pltpu.VMEM((2 * HALF, 128), F32), pltpu.VMEM((HALF, 128), F32), pltpu.VMEM((NG, 32, 128), F32),
         pltpu.VMEM((NC, 2, 128), F32), pltpu.VMEM((2, 128), F32), pltpu.VMEM((NC, 2, 128), F32),
         pltpu.VMEM((NC, 2, 128), F32), pltpu.VMEM((NG, NC, 2, 128), F32),
         dma((9,)), dma((NE,)), dma((NE,)), dma((NE,)), dma((NE,)), dma((QUADS, NE)), dma((QUADS, NE)),
-        dma((FP,)), dma((FP,)), dma((FP, NY)), dma((FP, NY)), dma, dma, dma((NG,)), dma((NG,)), dma((NC,)), dma((NC,)),
+        dma((FP,)), dma((FP,)), dma((FP, NY)), dma((FP, NY)),
+        dma((YF, NY)), dma((YF, NY)), dma((YF,)), dma((YF,)), dma, dma, dma((NG,)), dma((NG,)), dma((NC,)), dma((NC,)),
         dma((NC,)), dma((NC,)), dma((NG,)), dma((NG,)), dma, dma,
     ]
     held = pl.pallas_call(

time: 103 us -> 96.3 us (0.935); the launches traced: 102 us -> 96.1 us
  Pallas kernels: 101 us -> 95.5 us
    pallas_call x1, Pallas kernels: 96.9 us -> 91.4 us  [local(): pl.pallas_call(kernel, out_shape=(jax.ShapeDtypeStruct((NE, CH, 128), BF)...]
where the time goes in v3:
time: 96.3 us; the launch traced here: 96.1 us
  Pallas kernels  95.5 us (99%)
    pallas_call x1, Pallas kernels, local(): pl.pallas_call(kernel, out_shape=(jax.ShapeDtypeStruct((NE, CH, 128), BF)...  91.4 us
    pallas_call x1, Pallas kernels, local(): pl.pallas_call(finish, out_shape=(jax.ShapeDtypeStruct((2, J, D, NF), BF)...  4.06 us

profile of v3, /device:TPU:6, one launch (start us, length us, event | category | flops | bytes accessed | tf_op | source)
XLA Modules:
  0.0 96.1 jit_solution(15197116490783045600)
XLA Ops:
  0.6 91.4 %layer_and_tables.1 = (bf16[32,144,128]{2,1,0:T(8,128)(2,1)}, f32[8,32,192]{2,1,0:T(8,128)}, f32[1024,128]{1,0:T(8,128)}) custom-call(bf16[12,192,256]{2,1,0:T(8,128)(2,1)} %bitcast.11, bf16[12,192,256]{2,1,0:T(8,128)(2,1)} %bitcast.12, s32[12,256]{1,0:T(8,128)} %now_hbm.1, s32[12,256]{1,0:T(8,128)} %next_hbm.1, bf16[8,192,512]{2,1,0:T(8,128)(2,1)} %bitcast.10, ...), custom_call_target="tpu_custom_call" | custom-call | tf_op jit(solution)/shard_map/layer_and_tables/pallas_call | solution.py:496
  92.0 4.1 %finish.1 = (bf16[2,6,192,256]{3,2,1,0:T(8,128)(2,1)}, f32[8,32,192]{2,1,0:T(8,128)}, f32[256,128]{1,0:T(8,128)}, f32[192,128]{1,0:T(8,128)}, f32[256,256]{1,0:T(8,128)}, /*index=5*/f32[1,192]{1,0:T(1,128)}) custom-call(bf16[32,144,128]{2,1,0:T(8,128)(2,1)} %get-tuple-element.15.recv_n, f32[8,32,192]{2,1,0:T(8,128)} %get-tuple-element.16.table, ...), custom_call_target="tpu_custom_call" | custom-call | tf_op jit(solution)/shard_map/finish/pallas_call | solution.py:512

commit v4 on v3

--- a/solution.py
+++ b/solution.py
@@ -52,7 +52,7 @@
     next_ref, now_ref, idt, ids_s, ids_r, now_k, next_k, main_f, tail_f,
     send_n, send_d, recv_d, part_s, part_x, part_y, part_r, part_z, part_t, part_w, part_v,
     gfm_t, gproj_t, glcb_t, ggain, wfm_t, wproj, gain_c,
-    dn_s, dn_p, dn_g, dn_c, dn_own, dn_c2, dn_row, dn_g2,
+    dn_s, dn_p, dn_g, dn_c, dn_own, dn_c2, dn_row, dn_row16, dn_g2,
     lsem, id_ss, id_rs, n_ss, n_rs, d_ss, d_rs, px_ss, px_rs, p_ss, p_rs, z_ss, z_rs, w_ss, w_rs,
     pr_ss, pr_rs, g1_ss, g1_rs, c1_ss, c1_rs, c2_ss, c2_rs, g2_ss, g2_rs, pl_ss, pl_rs,
 ):
@@ -354,11 +354,13 @@
 
     loop(1, NC, lambda k: c2_copy(chip, lax.rem(chip + NC - k, NC)).wait_recv())
 
+    dn_row16[...] = dn_row[...].reshape(32, 128).astype(BF)
+
     def g2_copy(t, s):
-        return grp_copy(dn_row, dn_g2.at[s], g2_ss.at[t], g2_rs.at[s], t)
+        return grp_copy(dn_row16, dn_g2.at[s], g2_ss.at[t], g2_rs.at[s], t)
 
     loop(1, NG, lambda k: g2_copy(lax.rem(g + k, NG), g).start())
-    dn_g2[g] = dn_row[...]
+    dn_g2[g] = dn_row16[...]
 
     for i in range(YF, FP):
         rows = slice(i * PR, (i + 1) * PR)
@@ -383,7 +385,7 @@
     def half(h, value):
         dn_full[pl.ds(pl.multiple_of(h * HALF, HALF), HALF), :] = value
 
-    half(core, dn_g2[...].reshape(HALF, 128))
+    half(core, dn_g2[...].astype(F32).reshape(HALF, 128))
     pair2 = emb_copy(
         dn_full.at[pl.ds(mine, HALF)], dn_full.at[pl.ds(mine, HALF)], pl_ss, pl_rs, mate, e)
     pair2.start()
@@ -487,7 +489,7 @@
         pltpu.VMEM((K, NF), BF), pltpu.VMEM((K, D), BF), pltpu.VMEM((D, 128), F32),
         pltpu.VMEM((2 * HALF, 128), F32), pltpu.VMEM((HALF, 128), F32), pltpu.VMEM((NG, 32, 128), F32),
         pltpu.VMEM((NC, 2, 128), F32), pltpu.VMEM((2, 128), F32), pltpu.VMEM((NC, 2, 128), F32),
-        pltpu.VMEM((NC, 2, 128), F32), pltpu.VMEM((NG, NC, 2, 128), F32),
+        pltpu.VMEM((NC, 2, 128), F32), pltpu.VMEM((32, 128), BF), pltpu.VMEM((NG, 32, 128), BF),
         dma((9,)), dma((NE,)), dma((NE,)), dma((NE,)), dma((NE,)), dma((QUADS, NE)), dma((QUADS, NE)),
         dma((FP,)), dma((FP,)), dma((FP, NY)), dma((FP, NY)),
         dma((YF, NY)), dma((YF, NY)), dma((YF,)), dma((YF,)), dma, dma, dma((NG,)), dma((NG,)), dma((NC,)), dma((NC,)),

time: 96.3 us -> 93.5 us (0.971)
  Pallas kernels: 95.5 us -> 92.7 us
    pallas_call x1, Pallas kernels: 91.4 us -> 88.6 us  [local(): pl.pallas_call(kernel, out_shape=(jax.ShapeDtypeStruct((NE, CH, 128), BF)...]
where the time goes in v4:
time: 93.5 us; the launch traced here: 93.3 us
  Pallas kernels  92.7 us (99%)
    pallas_call x1, Pallas kernels, local(): pl.pallas_call(kernel, out_shape=(jax.ShapeDtypeStruct((NE, CH, 128), BF)...  88.6 us
    pallas_call x1, Pallas kernels, local(): pl.pallas_call(finish, out_shape=(jax.ShapeDtypeStruct((2, J, D, NF), BF)...  4.06 us

profile of v4, /device:TPU:6, one launch (start us, length us, event | category | flops | bytes accessed | tf_op | source)
XLA Modules:
  0.0 93.3 jit_solution(2480499788717129603)
XLA Ops:
  0.6 88.6 %layer_and_tables.1 = (bf16[32,144,128]{2,1,0:T(8,128)(2,1)}, f32[8,32,192]{2,1,0:T(8,128)}, f32[1024,128]{1,0:T(8,128)}) custom-call(bf16[12,192,256]{2,1,0:T(8,128)(2,1)} %bitcast.11, bf16[12,192,256]{2,1,0:T(8,128)(2,1)} %bitcast.12, s32[12,256]{1,0:T(8,128)} %now_hbm.1, s32[12,256]{1,0:T(8,128)} %next_hbm.1, bf16[8,192,512]{2,1,0:T(8,128)(2,1)} %bitcast.10, ...), custom_call_target="tpu_custom_call" | custom-call | tf_op jit(solution)/shard_map/layer_and_tables/pallas_call | solution.py:498
  89.2 4.1 %finish.1 = (bf16[2,6,192,256]{3,2,1,0:T(8,128)(2,1)}, f32[8,32,192]{2,1,0:T(8,128)}, f32[256,128]{1,0:T(8,128)}, f32[192,128]{1,0:T(8,128)}, f32[256,256]{1,0:T(8,128)}, /*index=5*/f32[1,192]{1,0:T(1,128)}) custom-call(bf16[32,144,128]{2,1,0:T(8,128)(2,1)} %get-tuple-element.15.recv_n, f32[8,32,192]{2,1,0:T(8,128)} %get-tuple-element.16.table, ...), custom_call_target="tpu_custom_call" | custom-call | tf_op jit(solution)/shard_map/finish/pallas_call | solution.py:514
